TPU v7x, 128 devices: a whole 4x4x4 slice. The times are simulated.
128 devices in a mesh: section: 2 (over z_lo), dp: 8 (over y, core), tensor: 8 (over z_hi, x).
Axes of the slice: x: 4, y: 4, z: 4 (z_hi: 2, z_lo: 2; z = z_hi * 2 + z_lo), core: 2. Of those that a mesh axis runs over, the one named last changes fastest.
Arguments:
- inputs: bfloat16 [384, 8192], P('tensor', 'dp'), may hold values from -6 to 6
- cotangent: bfloat16 [384, 8192], P('tensor', 'dp'), may hold values from -1.5 to 1.5
- gate_weight: bfloat16 [2, 8192, 14336], P('section', 'dp', 'tensor'), may hold values from -0.0625 to 0.0625
- up_weight: bfloat16 [2, 8192, 14336], P('section', 'dp', 'tensor'), may hold values from -0.0625 to 0.0625
- down_weight: bfloat16 [2, 14336, 8192], P('section', 'tensor', 'dp'), may hold values from -0.046875 to 0.046875
Outputs:
- section_out: bfloat16 [2, 384, 8192], P('section', 'tensor', 'dp')
- input_grad: bfloat16 [2, 384, 8192], P('section', 'tensor', 'dp')
- gate_grad: bfloat16 [2, 8192, 14336], P('section', 'dp', 'tensor')
- up_grad: bfloat16 [2, 8192, 14336], P('section', 'dp', 'tensor')
- down_grad: bfloat16 [2, 14336, 8192], P('section', 'tensor', 'dp')
All inputs are finite; a program needn't handle non-finite values.
Results may differ from a plain program's by a relative error of at most 0.015.
Values may be sent and summed in bfloat16 or wider, within the bound.
A program may use at most 128 MiB of HBM per device.

v0:
```python
import jax
import jax.numpy as jnp
from jax import lax
from jax.sharding import PartitionSpec as P


def shifted(value, axis, steps):
    count = lax.axis_size(axis)
    initial, last = (max(0, -steps), min(count, count - steps))
    return lax.ppermute(value, axis, [(source, source + steps) for source in range(initial, last)])


def contract_first(left, right):
    return lax.dot_general(
        left, right, (((0,), (0,)), ((), ())), preferred_element_type=jnp.float32
    )


def contract_last(left, right):
    return lax.dot_general(
        left, right, (((1,), (1,)), ((), ())), preferred_element_type=jnp.float32
    )


def gate_grads(grad_hidden, gate_pre, up_pre):
    sigma = jax.nn.sigmoid(gate_pre)
    grad_gate = (grad_hidden * up_pre * sigma * (1.0 + gate_pre * (1.0 - sigma))).astype(
        jnp.bfloat16
    )
    grad_up = (grad_hidden * gate_pre * sigma).astype(jnp.bfloat16)
    return (grad_gate, grad_up)


def per_device(inputs, cotangent, gate_weight, up_weight, down_weight):
    w_gate = gate_weight[0]
    w_up = up_weight[0]
    w_down = down_weight[0]
    edge_rows = inputs.shape[0]
    section_index = lax.axis_index("section")

    def gather_rows(shard):
        return lax.all_gather(shard, "tensor", axis=0, tiled=True)

    def tensor_sum(term_fn):
        return lax.psum_scatter(
            term_fn(jnp.int32(0), edge_rows * lax.axis_size("tensor")),
            "tensor",
            scatter_dimension=0,
            tiled=True,
        )

    def relay(block, offset):
        return shifted(block, "section", offset)

    def forward(full_in, edge_in):
        gate_term = jnp.dot(full_in, w_gate, preferred_element_type=jnp.float32)
        up_term = jnp.dot(full_in, w_up, preferred_element_type=jnp.float32)
        gate_pre, up_pre = lax.psum((gate_term, up_term), "dp")
        hidden = (jax.nn.silu(gate_pre) * up_pre).astype(jnp.bfloat16)

        def down_term(start, count):
            return jnp.dot(hidden, w_down, preferred_element_type=jnp.float32)

        edge_out = (edge_in.astype(jnp.float32) + tensor_sum(down_term)).astype(jnp.bfloat16)
        return (edge_out, gate_pre, up_pre, hidden)

    def backward(full_in, edge_grad, gate_pre, up_pre, hidden):
        full_grad = gather_rows(edge_grad)
        down_part = contract_first(hidden, full_grad).astype(jnp.bfloat16)
        grad_term = contract_last(full_grad, w_down)
        grad_hidden = lax.psum(grad_term, "dp")
        grad_gate, grad_up = gate_grads(grad_hidden, gate_pre, up_pre)
        gate_part = contract_first(full_in, grad_gate).astype(jnp.bfloat16)
        up_part = contract_first(full_in, grad_up).astype(jnp.bfloat16)

        def back_term(start, count):
            return contract_last(grad_gate, w_gate) + contract_last(grad_up, w_up)

        edge_in_grad = (edge_grad.astype(jnp.float32) + tensor_sum(back_term)).astype(jnp.bfloat16)
        return (edge_in_grad, (gate_part, up_part, down_part))

    inputs_full = gather_rows(inputs)
    first_shard, gate_first, up_first, hidden_first = forward(inputs_full, inputs)
    second_edge = relay(first_shard, 1)
    second_full = gather_rows(second_edge)
    second_shard, gate_second, up_second, hidden_second = forward(second_full, second_edge)
    mid_shard, parts_two = backward(second_full, cotangent, gate_second, up_second, hidden_second)
    mid_edge = relay(mid_shard, -1)
    start_shard, parts_one = backward(inputs_full, mid_edge, gate_first, up_first, hidden_first)
    first_section = section_index == 0
    section_out = jnp.where(first_section, first_shard, second_shard)[None]
    input_grad = jnp.where(first_section, start_shard, mid_shard)[None]
    gate_grad = jnp.where(first_section, parts_one[0], parts_two[0])[None]
    up_grad = jnp.where(first_section, parts_one[1], parts_two[1])[None]
    down_grad = jnp.where(first_section, parts_one[2], parts_two[2])[None]
    return (section_out, input_grad, gate_grad, up_grad, down_grad)


def solution(mesh):
    in_specs = (
        P("tensor", "dp"),
        P("tensor", "dp"),
        P("section", "dp", "tensor"),
        P("section", "dp", "tensor"),
        P("section", "tensor", "dp"),
    )
    out_specs = (
        P("section", "tensor", "dp"),
        P("section", "tensor", "dp"),
        P("section", "dp", "tensor"),
        P("section", "dp", "tensor"),
        P("section", "tensor", "dp"),
    )
    return jax.shard_map(
        per_device, mesh=mesh, in_specs=in_specs, out_specs=out_specs, check_vma=False
    )
```

profile of v0, /device:TPU:1, one launch (start us, length us, event | category | flops | bytes accessed | tf_op | source)
XLA Modules:
  0.0 733.4 jit_solution(4982493936418003457)
XLA Ops:
  7.2 32.6 %all_gather.12 = bf16[384,1024]{1,0:T(8,128)(2,1)S(1)} all-gather(bf16[48,1024]{1,0:T(8,128)(2,1)} %param.5), channel_id=1, replica_groups=mesh['section'=2,'dp'=8,'tensor'=8] {'tensor'}, dimensions={0}, use_global_device_ids=true | all-gather | bytes 884736 | tf_op jit(solution)/shard_map/all_gather | solution.py:42
  39.8 5.3 fusion.16
  48.3 84.6 %all-reduce.10.cloned.1.call-done = (f32[384,1792]{1,0:T(8,128)}, f32[384,1792]{1,0:T(8,128)}) async-done(((f32[384,1792]{1,0:T(8,128)}, f32[384,1792]{1,0:T(8,128)}), (f32[384,1792]{1,0:T(8,128)}, f32[384,1792]{1,0:T(8,128)})) %all-reduce.10.cloned.1.call-update) | async-done | bytes 5505040 | tf_op jit(solution)/shard_map/psum | solution.py:58
  140.3 32.0 %all_gather.14 = bf16[384,1024]{1,0:T(8,128)(2,1)S(1)} all-gather(bf16[48,1024]{1,0:T(8,128)(2,1)S(1)} %copy-done.17), channel_id=1, replica_groups=mesh['section'=2,'dp'=8,'tensor'=8] {'tensor'}, dimensions={0}, use_global_device_ids=true | all-gather | bytes 884736 | tf_op jit(solution)/shard_map/all_gather | solution.py:42
  172.4 42.5 %reduce-scatter.5.cloned.1.call-done = f32[48,1024]{1,0:T(8,128)} async-done(((f32[384,1024]{1,0:T(8,128)}), f32[48,1024]{1,0:T(8,128)}) %reduce-scatter.5.cloned.1.call-update) | async-done | bytes 196624 | tf_op jit(solution)/shard_map/reduce_scatter | solution.py:45
  218.5 5.2 fusion.4
  223.7 30.4 %all_gather.13 = bf16[384,1024]{1,0:T(8,128)(2,1)S(1)} all-gather(bf16[48,1024]{1,0:T(8,128)(2,1)S(1)} %collective-permute-done), channel_id=1, replica_groups=mesh['section'=2,'dp'=8,'tensor'=8] {'tensor'}, dimensions={0}, use_global_device_ids=true | all-gather | bytes 884736 | tf_op jit(solution)/shard_map/all_gather | solution.py:42
  260.6 108.7 %all-reduce.8.cloned.1.call-done = (f32[384,1792]{1,0:T(8,128)}, f32[384,1792]{1,0:T(8,128)}, f32[384,1792]{1,0:T(8,128)}) async-done(((f32[384,1792]{1,0:T(8,128)}, f32[384,1792]{1,0:T(8,128)}, f32[384,1792]{1,0:T(8,128)}), (f32[384,1792]{1,0:T(8,128)}, f32[384,1792]{1,0:T(8,128)}, f32[384,1792]{1,0:T(8,128)})) %all-reduce.8.cloned.1.call-update) | async-done | bytes 8257552 | tf_op jit(solution)/shard_map/psum | solution.py:58
  369.3 5.2 multiply_convert_fusion.3
  380.4 73.5 %reduce-scatter.9.cloned.1.call-done = f32[48,1024]{1,0:T(8,128)} async-done(((f32[384,1024]{1,0:T(8,128)}), f32[48,1024]{1,0:T(8,128)}) %reduce-scatter.9.cloned.1.call-update) | async-done | bytes 196624 | tf_op jit(solution)/shard_map/reduce_scatter | solution.py:45
  456.2 4.1 collective-permute-done.1
  460.9 29.9 %all_gather.15 = bf16[384,1024]{1,0:T(8,128)(2,1)S(1)} all-gather(bf16[48,1024]{1,0:T(8,128)(2,1)S(1)} %collective-permute-done.1), channel_id=1, replica_groups=mesh['section'=2,'dp'=8,'tensor'=8] {'tensor'}, dimensions={0}, use_global_device_ids=true | all-gather | bytes 884736 | tf_op jit(solution)/shard_map/all_gather | solution.py:42
  491.6 5.2 fusion.2
  496.9 5.3 fusion.6
  502.6 66.5 %all-reduce.6.cloned.1.call-done = f32[384,1792]{1,0:T(8,128)} async-done(((f32[384,1792]{1,0:T(8,128)}), f32[384,1792]{1,0:T(8,128)}) %all-reduce.6.cloned.1.call-update) | async-done | bytes 2752528 | tf_op jit(solution)/shard_map/psum | solution.py:71
  569.1 4.0 multiply_convert_fusion.1
  579.0 5.2 convolution_convert_fusion
  584.2 63.9 %reduce-scatter.7.cloned.1.call-done = f32[48,1024]{1,0:T(8,128)} async-done(((f32[384,1024]{1,0:T(8,128)}), f32[48,1024]{1,0:T(8,128)}) %reduce-scatter.7.cloned.1.call-update) | async-done | bytes 196624 | tf_op jit(solution)/shard_map/reduce_scatter | solution.py:45
  649.8 5.2 select_bitcast_fusion
  657.1 4.0 fusion
  661.2 6.0 copy.13
  669.3 4.0 fusion.1
  673.3 6.0 copy.12
  679.3 45.6 %reduce-scatter.11.cloned.1.call-done = f32[48,1024]{1,0:T(8,128)} async-done(((f32[384,1024]{1,0:T(8,128)}), f32[48,1024]{1,0:T(8,128)}) %reduce-scatter.11.cloned.1.call-update) | async-done | bytes 196624 | tf_op jit(solution)/shard_map/reduce_scatter | solution.py:45
  (96 shorter events, 44.0 us)
Async XLA Ops:
  7.2 125.7 %all-reduce.10.cloned.1.call-start = ((), (), s32[]{:S(2)}) async-start(), calls=%async_computation.10 | async-start | bytes 11010048 | tf_op jit(solution)/shard_map/psum | solution.py:58
  39.8 5.3 copy-start.28
  48.2 166.7 %reduce-scatter.5.cloned.1.call-start = ((), (), s32[]{:S(2)}) async-start(), calls=%async_computation.4 | async-start | bytes 1769472 | tf_op jit(solution)/shard_map/reduce_scatter | solution.py:45
  132.9 4.6 copy-start.24
  137.5 77.4 %copy-start.16 = (bf16[48,1024]{1,0:T(8,128)(2,1)S(1)}, bf16[48,1024]{1,0:T(8,128)(2,1)}, u32[]{:S(2)}) copy-start(bf16[48,1024]{1,0:T(8,128)(2,1)} %param.5) | copy-start | bytes 294916
  140.3 229.1 %all-reduce.8.cloned.1.call-start = ((), (), s32[]{:S(2)}) async-start(), calls=%async_computation.9 | async-start | bytes 16515072 | tf_op jit(solution)/shard_map/psum | solution.py:58
  172.4 51.3 %copy-start.14 = (bf16[384,1024]{1,0:T(8,128)(2,1)}, bf16[384,1024]{1,0:T(8,128)(2,1)S(1)}, u32[]{:S(2)}) copy-start(bf16[384,1024]{1,0:T(8,128)(2,1)S(1)} %all_gather.14) | copy-start | bytes 2359300
  215.9 7.8 %copy-start.21 = (bf16[48,1024]{1,0:T(8,128)(2,1)}, bf16[48,1024]{1,0:T(8,128)(2,1)S(1)}, u32[]{:S(2)}) copy-start(bf16[48,1024]{1,0:T(8,128)(2,1)S(1)} %add_convert_fusion.3) | copy-start | bytes 294916
  215.9 38.2 %copy-start.25 = (bf16[1,1024,1792]{2,1,0:T(8,128)(2,1)S(1)}, bf16[1,1024,1792]{2,1,0:T(8,128)(2,1)}, u32[]{:S(2)}) copy-start(bf16[1,1024,1792]{2,1,0:T(8,128)(2,1)} %param.8) | copy-start | bytes 11010052
  215.9 7.8 %collective-permute-start = (bf16[48,1024]{1,0:T(8,128)(2,1)S(1)}, bf16[48,1024]{1,0:T(8,128)(2,1)S(1)}, u32[]{:S(2)}, u32[]{:S(2)}) collective-permute-start(bf16[48,1024]{1,0:T(8,128)(2,1)S(1)} %add_convert_fusion.3), channel_id=1, source_target_pairs={{0,64},{1,65},{2,66},{3,67},{4,68},{5,69},{6,70},{7,71},{8,72},{9,... | collective-permute-start | bytes 294920 | tf_op jit(solution)/shard_map/ppermute | solution.py:10
  223.7 33.6 %copy-start.18 = (bf16[48,1024]{1,0:T(8,128)(2,1)}, bf16[48,1024]{1,0:T(8,128)(2,1)S(1)}, u32[]{:S(2)}) copy-start(bf16[48,1024]{1,0:T(8,128)(2,1)S(1)} %collective-permute-done) | copy-start | bytes 294916
  260.4 193.5 %reduce-scatter.9.cloned.1.call-start = ((), (), s32[]{:S(2)}) async-start(), calls=%async_computation.6 | async-start | bytes 1769472 | tf_op jit(solution)/shard_map/reduce_scatter | solution.py:45
  369.3 5.2 copy-start.26
  380.3 188.7 %all-reduce.6.cloned.1.call-start = ((), (), s32[]{:S(2)}) async-start(), calls=%async_computation.7 | async-start | bytes 5505024 | tf_op jit(solution)/shard_map/psum | solution.py:71
  454.9 42.1 %copy-start.22 = (bf16[48,1024]{1,0:T(8,128)(2,1)}, bf16[48,1024]{1,0:T(8,128)(2,1)S(1)}, u32[]{:S(2)}) copy-start(bf16[48,1024]{1,0:T(8,128)(2,1)S(1)} %add_convert_fusion.1) | copy-start | bytes 294916
  454.9 5.4 collective-permute-start.1
  496.9 151.2 %reduce-scatter.7.cloned.1.call-start = ((), (), s32[]{:S(2)}) async-start(), calls=%async_computation.5 | async-start | bytes 1769472 | tf_op jit(solution)/shard_map/reduce_scatter | solution.py:45
  496.9 72.2 %copy-start = (f32[384,1792]{1,0:T(8,128)S(1)}, f32[384,1792]{1,0:T(8,128)}, u32[]{:S(2)}) copy-start(f32[384,1792]{1,0:T(8,128)} %get-tuple-element.13) | copy-start | bytes 8257540
  502.3 222.6 %reduce-scatter.11.cloned.1.call-start = ((), (), s32[]{:S(2)}) async-start(), calls=%async_computation.8 | async-start | bytes 1769472 | tf_op jit(solution)/shard_map/reduce_scatter | solution.py:45
  579.0 70.8 %copy-start.7 = (bf16[384,1792]{1,0:T(8,128)(2,1)S(1)}, bf16[384,1792]{1,0:T(8,128)(2,1)}, u32[]{:S(2)}) copy-start(bf16[384,1792]{1,0:T(8,128)(2,1)} %copy-done.6) | copy-start | bytes 4128772
  649.8 5.2 copy-start.11
  661.2 6.0 copy-start.9
  673.3 51.6 %copy-start.20 = (bf16[48,1024]{1,0:T(8,128)(2,1)S(1)}, bf16[48,1024]{1,0:T(8,128)(2,1)}, u32[]{:S(2)}) copy-start(bf16[48,1024]{1,0:T(8,128)(2,1)} %copy-done.19) | copy-start | bytes 294916
  673.3 51.6 %copy-start.23 = (bf16[48,1024]{1,0:T(8,128)(2,1)S(1)}, bf16[48,1024]{1,0:T(8,128)(2,1)}, u32[]{:S(2)}) copy-start(bf16[48,1024]{1,0:T(8,128)(2,1)} %copy-done.22) | copy-start | bytes 294916
  (17 other events, 37.7 us)
Sparse Core Ops, SparseCore 0:
  48.4 84.4 all-reduce.9
  140.4 74.4 reduce-scatter.4
  260.5 108.7 all-reduce.7
  380.5 73.3 reduce-scatter.8
  497.0 72.0 all-reduce.5
  573.3 74.7 reduce-scatter.6
  651.8 73.0 reduce-scatter.10
where the time goes:
time: 734 us; the launch traced here: 733 us
  waiting for transfers between devices  490 us (67%)
  blocking collectives  125 us (17%)
  matrix products  64.6 us (9%)
  other arithmetic  18 us (2%)
  local copies, waits for them, and re-layouts  17.5 us (2%)
  between operations  14.4 us (2%)
    reduce_scatter x4, waiting for transfers between devices, tensor_sum(): lax.psum_scatter(term_fn(jnp.int32(0), edge_rows * lax.axis_size('tensor'...  226 us
    psum x2, waiting for transfers between devices, forward(): gate_pre, up_pre = lax.psum((gate_term, up_term), 'dp')  193 us
    all_gather x4, blocking collectives, gather_rows(): return lax.all_gather(shard, 'tensor', axis=0, tiled=True)  125 us
    psum x1, waiting for transfers between devices, backward(): grad_hidden = lax.psum(grad_term, 'dp')  66.5 us
    dot_general x6, matrix products, contract_first(): lax.dot_general(left, right, (((0,), (0,)), ((), ())), preferred_element_...  22.6 us
    dot_general x6, matrix products, contract_last(): lax.dot_general(left, right, (((1,), (1,)), ((), ())), preferred_element_...  19.2 us
    unnamed x66, local copies, waits for them, and re-layouts  17.5 us
  transfers between devices with their start and end apart: 9, of which 8 were waited for; matrix products, arithmetic and copies ran while one was open for 8% of the time, Pallas kernels for 0%

commit v1 on v0

v1 whole, which is shorter than its diff:
```python
import jax
import jax.numpy as jnp
from jax import lax
from jax.experimental import pallas as pl
from jax.experimental.pallas import tpu as pltpu
from jax.sharding import PartitionSpec as P

MESH = pl.DeviceIdType.MESH
F32 = jnp.float32
BF16 = jnp.bfloat16

D = 1024
HID = 1792
HC = HID // 2
TB = 48
HT = 4 * TB

BUFFERS = {
    "wg": ((D, HID), BF16),
    "wu": ((D, HID), BF16),
    "wd": ((HID, D), BF16),
    "u": ((2, 4, TB, D), BF16),
    "g": ((2, 4, TB, D), BF16),
    "hid": ((2, 4, TB, HID), BF16),
    "grad": ((2, 4, 2, TB, HID), BF16),
    "fac": ((2, 4, 2, TB, HID), BF16),
    "gh": ((2, 4, TB, HID), BF16),
    "f_psend": ((2, 2, 4, TB, HC), BF16),
    "f_precv": ((2, 2, 4, TB, HC), BF16),
    "f_own": ((2, 2, 4, TB, HC), F32),
    "f_ysend": ((2, 3, 2, TB, HC), BF16),
    "f_yrecv": ((2, 3, 2, TB, HC), BF16),
    "b_psend": ((2, 1, 4, TB, HC), BF16),
    "b_precv": ((2, 1, 4, TB, HC), BF16),
    "b_own": ((2, 1, 4, TB, HC), F32),
    "b_ysend": ((2, 3, 1, TB, HC), BF16),
    "b_yrecv": ((2, 3, 1, TB, HC), BF16),
    "ghown": ((2, TB, HC), F32),
    "xsend": ((2, 2, 4, TB, D), BF16),
    "xown": ((2, 2, 4, TB, D), F32),
    "xrecv": ((2, 2, 3, TB, D), BF16),
    "zsend": ((2, TB, D), BF16),
    "zrecv": ((2, 2, TB, D), BF16),
    "home": ((TB, D), BF16),
    "zzsend": ((TB, D), BF16),
    "zzrecv": ((TB, D), BF16),
    "og": ((D, HID), BF16),
    "ou": ((D, HID), BF16),
    "od": ((HID, D), BF16),
}


def slot_table():
    names = []
    names += [("near", 0, k) for k in (1, 2, 3)] + [("cross", 0, k) for k in range(4)]
    for h in range(2):
        for p in ("f", "b"):
            names.append((p + "pair", h))
            names += [(p + "y", h, k) for k in (1, 2, 3)]
        for a in ("hid", "grad", "fac", "gh"):
            names += [(a + "y", h, k) for k in (1, 2, 3)]
            names += [(a + "p", h, k) for k in range(4)]
        for tag in range(2):
            names += [("x", tag, h, k) for k in (1, 2, 3)]
        names += [("z", h, 0), ("z", h, 1)]
        names += [("xg", h, k) for k in (1, 2, 3)]
    names += [("home",), ("zz",)]
    return {name: i for i, name in enumerate(names)}


SLOTS = slot_table()


def tiles(total, width=256):
    return [(o, min(width, total - o)) for o in range(0, total, width)]


def dot_nn(a, b):
    return lax.dot_general(a, b, (((1,), (0,)), ((), ())), preferred_element_type=F32)


def dot_nt(a, b):
    return lax.dot_general(a, b, (((1,), (1,)), ((), ())), preferred_element_type=F32)


def dot_tn(a, b):
    return lax.dot_general(a, b, (((0,), (0,)), ((), ())), preferred_element_type=F32)


def kernel(in_ref, ct_ref, wg_hbm, wu_hbm, wd_hbm, so_ref, ig_ref, og_hbm, ou_hbm, od_hbm, *scratch):
    b = dict(zip(BUFFERS, scratch))
    send_sem, recv_sem, load_sem, out_sem = scratch[len(BUFFERS):]
    s, d, t = lax.axis_index("section"), lax.axis_index("dp"), lax.axis_index("tensor")
    y, c = d // 2, d % 2
    zh, x = t // 4, t % 4

    def ring(v, k):
        return (v + k) % 4

    def at_y(k):
        return {"dp": ring(y, k) * 2 + c}

    def at_x(k):
        return {"tensor": zh * 4 + ring(x, k)}

    def at_cross(k):
        return {"section": 1 - s, "tensor": (1 - zh) * 4 + ring(x, k)}

    def at_other(z):
        return {"section": 1 - s, "tensor": z * 4 + x}

    pair = {"dp": y * 2 + 1 - c}
    zz_peer = {"tensor": (1 - zh) * 4 + x}
    same = {"section": 1 - s}
    col = pl.multiple_of(c * HC, 128)
    col_other = pl.multiple_of((1 - c) * HC, 128)

    weights = {}
    for i, (name, src) in enumerate((("wg", wg_hbm), ("wu", wu_hbm), ("wd", wd_hbm))):
        weights[name] = pltpu.make_async_copy(src, b[name], load_sem.at[i])
        weights[name].start()

    barrier = pltpu.get_barrier_semaphore()
    peers = [pair, zz_peer, same]
    peers += [at_y(k) for k in (1, 2, 3)] + [at_x(k) for k in (1, 2, 3)]
    peers += [at_cross(k) for k in range(4)]
    for peer in peers:
        pl.semaphore_signal(barrier, 1, device_id=peer, device_id_type=MESH)
    pl.semaphore_wait(barrier, len(peers))

    def role(first):
        sent = []
        outs = []

        def send(slot, src, dst, peer):
            i = SLOTS[slot]
            copy = pltpu.make_async_remote_copy(
                src_ref=src, dst_ref=dst, send_sem=send_sem.at[i], recv_sem=recv_sem.at[i],
                device_id=peer, device_id_type=MESH,
            )
            copy.start()
            sent.append(copy)

        def arrived(slot, dst):
            i = SLOTS[slot]
            pltpu.make_async_remote_copy(
                src_ref=dst, dst_ref=dst, send_sem=send_sem.at[i], recv_sem=recv_sem.at[i],
                device_id=pair, device_id_type=MESH,
            ).wait_recv()

        mine, theirs = (in_ref, ct_ref) if first else (ct_ref, in_ref)
        full, full_there = (b["u"], b["g"]) if first else (b["g"], b["u"])

        def send_near():
            for k in (2, 1, 3):
                send(("near", 0, k), mine, full.at[zh, x], at_x(k))

        def send_cross():
            for k in (2, 1, 3, 0):
                send(("cross", 0, k), theirs, full_there.at[zh, x], at_cross(k))

        def gather_wait():
            for k in (1, 2, 3):
                arrived(("near", 0, k), full.at[zh, ring(x, 4 - k)])
            for k in range(4):
                arrived(("cross", 0, k), full.at[1 - zh, ring(x, 4 - k)])

        def mm_forward(h):
            u = b["u"][h].reshape(HT, D)
            for dst, start in ((b["f_psend"], col_other), (b["f_own"], col)):
                for a, w in enumerate((b["wg"], b["wu"])):
                    for o, n in tiles(HC):
                        r = dot_nn(u, w[:, pl.ds(pl.multiple_of(start + o, 128), n)])
                        dst[h, a, :, :, o:o + n] = r.reshape(4, TB, n).astype(dst.dtype)
                if dst is b["f_psend"]:
                    send(("fpair", h), dst.at[h], b["f_precv"].at[h], pair)

        def mm_hidden(h):
            g = b["g"][h].reshape(HT, D)
            for dst, start in ((b["b_psend"], col_other), (b["b_own"], col)):
                for o, n in tiles(HC):
                    r = dot_nt(g, b["wd"][pl.ds(pl.multiple_of(start + o, 128), n), :])
                    dst[h, 0, :, :, o:o + n] = r.reshape(4, TB, n).astype(dst.dtype)
                if dst is b["b_psend"]:
                    send(("bpair", h), dst.at[h], b["b_precv"].at[h], pair)

        def pair_add(p, h):
            own, prec, ysend, yrecv = (b[p + n] for n in ("_own", "_precv", "_ysend", "_yrecv"))
            arrived((p + "pair", h), prec.at[h])
            for k in (2, 1, 3):
                j = ring(y, k)
                for a in range(own.shape[1]):
                    ysend[h, k - 1, a] = (own[h, a, j] + prec[h, a, j].astype(F32)).astype(BF16)
                send((p + "y", h, k), ysend.at[h, k - 1], yrecv.at[h, k - 1], at_y(k))

        def y_sum(p, h):
            own, prec, yrecv = (b[p + n] for n in ("_own", "_precv", "_yrecv"))
            total = [own[h, a, y] + prec[h, a, y].astype(F32) for a in range(own.shape[1])]
            for k in (1, 3, 2):
                arrived((p + "y", h, k), yrecv.at[h, k - 1])
            for k in (1, 2, 3):
                total = [v + yrecv[h, k - 1, a].astype(F32) for a, v in enumerate(total)]
            return total

        def block(name, h, j, start):
            ref = b[name]
            cols = pl.ds(start, HC)
            return ref.at[h, j, :, :, cols] if len(ref.shape) == 5 else ref.at[h, j, :, cols]

        def spread(name, h):
            ref = block(name, h, y, col)
            for k in (2, 1, 3):
                send((name + "y", h, k), ref, ref, at_y(k))
            send((name + "p", h, 0), ref, ref, pair)

        def forward_pair(name, h):
            for k in (1, 3, 2):
                ref = block(name, h, ring(y, 4 - k), col)
                arrived((name + "y", h, k), ref)
                send((name + "p", h, k), ref, ref, pair)

        def pair_wait(name, h):
            for k in (0, 1, 3, 2):
                arrived((name + "p", h, k), block(name, h, ring(y, 4 - k), col_other))

        def x_scatter(tag, h, term):
            for o, n in tiles(D):
                r = term(o, n).reshape(4, TB, n)
                b["xown"][tag, h, :, :, o:o + n] = r
                b["xsend"][tag, h, :, :, o:o + n] = r.astype(BF16)
            for k in (2, 1, 3):
                send(("x", tag, h, k), b["xsend"].at[tag, h, ring(x, k)], b["xrecv"].at[tag, h, k - 1], at_x(k))

        def x_sum(tag, h):
            for k in (1, 3, 2):
                arrived(("x", tag, h, k), b["xrecv"].at[tag, h, k - 1])
            total = b["xown"][tag, h, x]
            for k in (1, 2, 3):
                total = total + b["xrecv"][tag, h, k - 1].astype(F32)
            return total

        def down(tag, h):
            hid = b["hid"][h].reshape(HT, HID)
            x_scatter(tag, h, lambda o, n: dot_nn(hid, b["wd"][:, o:o + n]))

        def back(tag, h):
            gg = b["grad"][h, :, 0].reshape(HT, HID)
            gu = b["grad"][h, :, 1].reshape(HT, HID)
            x_scatter(tag, h, lambda o, n: dot_nt(gg, b["wg"][o:o + n, :]) + dot_nt(gu, b["wu"][o:o + n, :]))

        def to_next(tag, h, residual):
            total = x_sum(tag, h) + jnp.where(zh == h, residual[...].astype(F32), 0.0)
            b["zsend"][h] = total.astype(BF16)
            send_z(h)

        def send_z(h):
            for z in range(2):
                i = SLOTS[("z", h, 0)] + zh
                copy = pltpu.make_async_remote_copy(
                    src_ref=b["zsend"].at[h], dst_ref=b["zrecv"].at[h, zh],
                    send_sem=send_sem.at[SLOTS[("z", h, z)]], recv_sem=recv_sem.at[i],
                    device_id=at_other(z), device_id_type=MESH,
                )
                copy.start()
                sent.append(copy)

        def from_other(h, dst):
            for z in range(2):
                arrived(("z", h, z), b["zrecv"].at[h, z])
            total = b["zrecv"][h, 0].astype(F32) + b["zrecv"][h, 1].astype(F32)
            dst[h, x] = total.astype(BF16)
            for k in (2, 1, 3):
                send(("xg", h, k), dst.at[h, x], dst.at[h, x], at_x(k))

        def x_gathered(h, dst):
            for k in (1, 3, 2):
                arrived(("xg", h, k), dst.at[h, ring(x, 4 - k)])

        def finish(tag, residual, out_ref):
            for h in range(2):
                b["xown"][tag, h, x] = x_sum(tag, h)
            b["zzsend"][...] = b["xown"][tag, 1 - zh, x].astype(BF16)
            send(("zz",), b["zzsend"], b["zzrecv"], zz_peer)

        def finish_wait(tag, residual, out_ref):
            arrived(("zz",), b["zzrecv"])
            total = b["xown"][tag, zh, x] + b["zzrecv"][...].astype(F32) + residual[zh, x].astype(F32)
            out_ref[0] = total.astype(BF16)

        def weight_grad(lhs, rhs, stage, out, i):
            for o, n in tiles(stage.shape[0]):
                stage[o:o + n, :] = dot_tn(lhs(o, n), rhs()).astype(BF16)
            copy = pltpu.make_async_copy(stage, out, out_sem.at[i])
            copy.start()
            outs.append(copy)

        def down_grad():
            weight_grad(
                lambda o, n: b["hid"][:, :, :, o:o + n].reshape(2 * HT, n),
                lambda: b["g"][...].reshape(2 * HT, D), b["od"], od_hbm, 2,
            )

        def gate_grad(a):
            weight_grad(
                lambda o, n: b["u"][:, :, :, o:o + n].reshape(2 * HT, n),
                lambda: b["grad"][:, :, a].reshape(2 * HT, HID),
                (b["og"], b["ou"])[a], (og_hbm, ou_hbm)[a], a,
            )

        both = range(2)
        if first:
            send_near()
            send_cross()
            full[zh, x] = in_ref[...]
            weights["wg"].wait()
            weights["wu"].wait()
            gather_wait()
            for h in both:
                mm_forward(h)
            for h in both:
                pair_add("f", h)
            for h in both:
                gate, up = y_sum("f", h)
                sig = 1.0 / (1.0 + jnp.exp(-gate))
                b["hid"][h, y, :, pl.ds(col, HC)] = (gate * sig * up).astype(BF16)
                spread("hid", h)
                b["fac"][h, y, 0, :, pl.ds(col, HC)] = (up * sig * (1.0 + gate * (1.0 - sig))).astype(BF16)
                b["fac"][h, y, 1, :, pl.ds(col, HC)] = (gate * sig).astype(BF16)
            weights["wd"].wait()
            for h in both:
                forward_pair("hid", h)
            for h in both:
                pair_wait("hid", h)
                down(0, h)
            for h in both:
                to_next(0, h, in_ref)
            for h in both:
                spread("fac", h)
            for h in both:
                forward_pair("fac", h)
            for h in both:
                pair_wait("fac", h)
            arrived(("home",), b["home"])
            so_ref[0] = b["home"][...]
            for h in both:
                from_other(h, b["g"])
            send(("home",), b["g"].at[zh, x], b["home"], same)
            for h in both:
                x_gathered(h, b["g"])
                mm_hidden(h)
            for h in both:
                pair_add("b", h)
            down_grad()
            for h in both:
                (gh,) = y_sum("b", h)
                b["gh"][h, y, :, pl.ds(col, HC)] = gh.astype(BF16)
                spread("gh", h)
            for h in both:
                forward_pair("gh", h)
            for h in both:
                pair_wait("gh", h)
                for j in range(4):
                    gh = b["gh"][h, j].astype(F32)
                    for a in range(2):
                        b["grad"][h, j, a] = (gh * b["fac"][h, j, a].astype(F32)).astype(BF16)
                back(1, h)
            gate_grad(0)
            finish(1, b["g"], ig_ref)
            gate_grad(1)
            finish_wait(1, b["g"], ig_ref)
        else:
            send_cross()
            send_near()
            full[zh, x] = ct_ref[...]
            weights["wd"].wait()
            gather_wait()
            for h in both:
                mm_hidden(h)
            for h in both:
                pair_add("b", h)
            for h in both:
                (b["ghown"][h],) = y_sum("b", h)
            weights["wg"].wait()
            weights["wu"].wait()
            for h in both:
                from_other(h, b["u"])
            send(("home",), b["u"].at[zh, x], b["home"], same)
            for h in both:
                x_gathered(h, b["u"])
                mm_forward(h)
            for h in both:
                pair_add("f", h)
            for h in both:
                gate, up = y_sum("f", h)
                sig = 1.0 / (1.0 + jnp.exp(-gate))
                gh = b["ghown"][h]
                grad_gate = gh * up * sig * (1.0 + gate * (1.0 - sig))
                b["grad"][h, y, 0, :, pl.ds(col, HC)] = grad_gate.astype(BF16)
                b["grad"][h, y, 1, :, pl.ds(col, HC)] = (gh * gate * sig).astype(BF16)
                spread("grad", h)
                b["hid"][h, y, :, pl.ds(col, HC)] = (gate * sig * up).astype(BF16)
            for h in both:
                forward_pair("grad", h)
            for h in both:
                pair_wait("grad", h)
                back(0, h)
            for h in both:
                to_next(0, h, ct_ref)
            for h in both:
                spread("hid", h)
            for h in both:
                forward_pair("hid", h)
            for h in both:
                pair_wait("hid", h)
                down(1, h)
            gate_grad(0)
            finish(1, b["u"], so_ref)
            gate_grad(1)
            down_grad()
            finish_wait(1, b["u"], so_ref)
            arrived(("home",), b["home"])
            ig_ref[0] = b["home"][...]
        for copy in sent:
            copy.wait_send()
        for copy in outs:
            copy.wait()

    pl.when(s == 0)(lambda: role(True))
    pl.when(s == 1)(lambda: role(False))


def per_device(inputs, cotangent, gate_weight, up_weight, down_weight):
    any_spec = pl.BlockSpec(memory_space=pl.ANY)
    vmem_spec = pl.BlockSpec(memory_space=pltpu.VMEM)
    n = len(SLOTS)
    outs = pl.pallas_call(
        kernel,
        out_shape=[
            jax.ShapeDtypeStruct((1, TB, D), BF16),
            jax.ShapeDtypeStruct((1, TB, D), BF16),
            jax.ShapeDtypeStruct((D, HID), BF16),
            jax.ShapeDtypeStruct((D, HID), BF16),
            jax.ShapeDtypeStruct((HID, D), BF16),
        ],
        in_specs=[vmem_spec, vmem_spec, any_spec, any_spec, any_spec],
        out_specs=[vmem_spec, vmem_spec, any_spec, any_spec, any_spec],
        scratch_shapes=[pltpu.VMEM(shape, dtype) for shape, dtype in BUFFERS.values()]
        + [
            pltpu.SemaphoreType.DMA((n,)),
            pltpu.SemaphoreType.DMA((n,)),
            pltpu.SemaphoreType.DMA((3,)),
            pltpu.SemaphoreType.DMA((3,)),
        ],
        compiler_params=pltpu.CompilerParams(
            collective_id=0, has_side_effects=True, vmem_limit_bytes=60 << 20
        ),
        name="sections",
    )(inputs, cotangent, gate_weight[0], up_weight[0], down_weight[0])
    return (outs[0], outs[1], outs[2][None], outs[3][None], outs[4][None])


def solution(mesh):
    in_specs = (
        P("tensor", "dp"),
        P("tensor", "dp"),
        P("section", "dp", "tensor"),
        P("section", "dp", "tensor"),
        P("section", "tensor", "dp"),
    )
    out_specs = (
        P("section", "tensor", "dp"),
        P("section", "tensor", "dp"),
        P("section", "dp", "tensor"),
        P("section", "dp", "tensor"),
        P("section", "tensor", "dp"),
    )
    return jax.shard_map(
        per_device, mesh=mesh, in_specs=in_specs, out_specs=out_specs, check_vma=False
    )
```

time: 734 us -> 177 us (0.24)
  waiting for transfers between devices: 490 us -> 0 us
  Pallas kernels: 0 us -> 164 us
  blocking collectives: 125 us -> 0 us
  matrix products: 64.6 us -> 0 us
  other arithmetic: 18 us -> 0 us
  between operations: 14.4 us -> 0.65 us
    psum x3 -> x0, waiting for transfers between devices: 260 us -> none  [the longest x2 193 us: forward(): gate_pre, up_pre = lax.psum((gate_term, up_term), 'dp')]
    reduce_scatter x4 -> x0, waiting for transfers between devices: 226 us -> none  [tensor_sum(): lax.psum_scatter(term_fn(jnp.int32(0), edge_rows * lax.axis_size('tensor'...]
    pallas_call x0 -> x1, Pallas kernels: none -> 164 us  [per_device(): pl.pallas_call(kernel, out_shape=[jax.ShapeDtypeStruct((1, TB, D), BF16),...]
    all_gather x4 -> x0, blocking collectives: 125 us -> none  [gather_rows(): return lax.all_gather(shard, 'tensor', axis=0, tiled=True)]
    dot_general x18 -> x0, matrix products: 64.6 us -> none  [the longest x6 22.6 us: contract_first(): lax.dot_general(left, right, (((0,), (0,)), ((), ())), preferred_element_...]
    convert_element_type x5 -> x0, other arithmetic: 14.6 us -> none  [the longest x2 9.21 us: gate_grads(): (grad_hidden * up_pre * sigma * (1.0 + gate_pre * (1.0 - sigma))).astype(...]
    unnamed x66 -> x9, local copies, waits for them, and re-layouts: 17.5 us -> 12.5 us
  transfers between devices with their start and end apart: 9 -> 0, of which waited for: 8 -> 0; matrix products, arithmetic and copies ran while one was open for 8% -> 0% of each run, Pallas kernels for 0% -> 0%
where the time goes in v1:
time: 177 us
  Pallas kernels  164 us (93%)
  local copies, waits for them, and re-layouts  12.5 us (7%)
    pallas_call x1, Pallas kernels, per_device(): pl.pallas_call(kernel, out_shape=[jax.ShapeDtypeStruct((1, TB, D), BF16),...  164 us
    unnamed x9, local copies, waits for them, and re-layouts  12.5 us

profile of v1, /device:TPU:1, one launch (start us, length us, event | category | flops | bytes accessed | tf_op | source)
XLA Modules:
  0.0 176.9 jit_solution(15218893050128639640)
XLA Ops:
  0.6 163.7 %sections.1 = (bf16[1,48,1024]{2,1,0:T(8,128)(2,1)}, bf16[1,48,1024]{2,1,0:T(8,128)(2,1)}, bf16[1024,1792]{1,0:T(8,128)(2,1)}, bf16[1024,1792]{1,0:T(8,128)(2,1)}, bf16[1792,1024]{1,0:T(8,128)(2,1)}) custom-call(bf16[48,1024]{1,0:T(8,128)(2,1)} %in_ref.1, bf16[48,1024]{1,0:T(8,128)(2,1)} %ct_ref.1, bf16[1024,1792]{1,0:T(8,128)(2,1)} %bitcast.9, ...), custom_call_target="tpu_custom_call" | custom-call | tf_op jit(solution)/shard_map/sections/pallas_call | solution.py:436
  164.4 1.5 copy.15
  165.9 1.5 copy.16
  167.4 0.0 copy-start.1
  167.4 4.3 %copy.17 = bf16[1,1024,1792]{2,1,0:T(8,128)(2,1)} copy(bf16[1,1024,1792]{2,1,0:T(8,128)(2,1)} %bitcast.8) | data formatting | bytes 7340032
  171.7 0.0 copy-done.1
  171.7 0.0 copy-start
  171.7 1.9 %copy.18 = bf16[1,1024,1792]{2,1,0:T(8,128)(2,1)} copy(bf16[1,1024,1792]{2,1,0:T(8,128)(2,1)S(1)} %bitcast.7) | data formatting | bytes 7340032
  173.6 1.5 copy-done
  175.1 1.8 %copy.19 = bf16[1,1792,1024]{2,1,0:T(8,128)(2,1)} copy(bf16[1,1792,1024]{2,1,0:T(8,128)(2,1)S(1)} %bitcast.6) | data formatting | bytes 7340032
Async XLA Ops:
  167.4 4.3 %copy-start.1 = (bf16[1024,1792]{1,0:T(8,128)(2,1)S(1)}, bf16[1024,1792]{1,0:T(8,128)(2,1)}, u32[]{:S(2)}) copy-start(bf16[1024,1792]{1,0:T(8,128)(2,1)} %get-tuple-element.13) | copy-start | bytes 11010052
  171.7 3.4 %copy-start = (bf16[1792,1024]{1,0:T(8,128)(2,1)S(1)}, bf16[1792,1024]{1,0:T(8,128)(2,1)}, u32[]{:S(2)}) copy-start(bf16[1792,1024]{1,0:T(8,128)(2,1)} %get-tuple-element.14) | copy-start | bytes 11010052

commit v2 on v1

--- a/solution.py
+++ b/solution.py
@@ -44,9 +44,6 @@
     "home": ((TB, D), BF16),
     "zzsend": ((TB, D), BF16),
     "zzrecv": ((TB, D), BF16),
-    "og": ((D, HID), BF16),
-    "ou": ((D, HID), BF16),
-    "od": ((HID, D), BF16),
 }
 
 
@@ -87,9 +84,9 @@
     return lax.dot_general(a, b, (((0,), (0,)), ((), ())), preferred_element_type=F32)
 
 
-def kernel(in_ref, ct_ref, wg_hbm, wu_hbm, wd_hbm, so_ref, ig_ref, og_hbm, ou_hbm, od_hbm, *scratch):
+def kernel(in_ref, ct_ref, wg_hbm, wu_hbm, wd_hbm, so_ref, ig_ref, og_ref, ou_ref, od_ref, *scratch):
     b = dict(zip(BUFFERS, scratch))
-    send_sem, recv_sem, load_sem, out_sem = scratch[len(BUFFERS):]
+    send_sem, recv_sem, load_sem = scratch[len(BUFFERS):]
     s, d, t = lax.axis_index("section"), lax.axis_index("dp"), lax.axis_index("tensor")
     y, c = d // 2, d % 2
     zh, x = t // 4, t % 4
@@ -117,7 +114,7 @@
 
     weights = {}
     for i, (name, src) in enumerate((("wg", wg_hbm), ("wu", wu_hbm), ("wd", wd_hbm))):
-        weights[name] = pltpu.make_async_copy(src, b[name], load_sem.at[i])
+        weights[name] = pltpu.make_async_copy(src.at[0], b[name], load_sem.at[i])
         weights[name].start()
 
     barrier = pltpu.get_barrier_semaphore()
@@ -130,7 +127,6 @@
 
     def role(first):
         sent = []
-        outs = []
 
         def send(slot, src, dst, peer):
             i = SLOTS[slot]
@@ -287,24 +283,21 @@
             total = b["xown"][tag, zh, x] + b["zzrecv"][...].astype(F32) + residual[zh, x].astype(F32)
             out_ref[0] = total.astype(BF16)
 
-        def weight_grad(lhs, rhs, stage, out, i):
-            for o, n in tiles(stage.shape[0]):
-                stage[o:o + n, :] = dot_tn(lhs(o, n), rhs()).astype(BF16)
-            copy = pltpu.make_async_copy(stage, out, out_sem.at[i])
-            copy.start()
-            outs.append(copy)
+        def weight_grad(lhs, rhs, out):
+            for o, n in tiles(out.shape[1]):
+                out[0, o:o + n, :] = dot_tn(lhs(o, n), rhs()).astype(BF16)
 
         def down_grad():
             weight_grad(
                 lambda o, n: b["hid"][:, :, :, o:o + n].reshape(2 * HT, n),
-                lambda: b["g"][...].reshape(2 * HT, D), b["od"], od_hbm, 2,
+                lambda: b["g"][...].reshape(2 * HT, D), od_ref,
             )
 
         def gate_grad(a):
             weight_grad(
                 lambda o, n: b["u"][:, :, :, o:o + n].reshape(2 * HT, n),
                 lambda: b["grad"][:, :, a].reshape(2 * HT, HID),
-                (b["og"], b["ou"])[a], (og_hbm, ou_hbm)[a], a,
+                (og_ref, ou_ref)[a],
             )
 
         both = range(2)
@@ -422,41 +415,52 @@
             ig_ref[0] = b["home"][...]
         for copy in sent:
             copy.wait_send()
-        for copy in outs:
-            copy.wait()
 
     pl.when(s == 0)(lambda: role(True))
     pl.when(s == 1)(lambda: role(False))
+
+
+def write_out(*refs):
+    sems = refs[-1]
+    half = len(refs) // 2
+    copies = []
+    for i, (src, dst) in enumerate(zip(refs[:half], refs[half:-1])):
+        copies.append(pltpu.make_async_copy(src, dst, sems.at[i]))
+        copies[-1].start()
+    for copy in copies:
+        copy.wait()
 
 
 def per_device(inputs, cotangent, gate_weight, up_weight, down_weight):
     any_spec = pl.BlockSpec(memory_space=pl.ANY)
     vmem_spec = pl.BlockSpec(memory_space=pltpu.VMEM)
     n = len(SLOTS)
+    shapes = [(1, TB, D), (1, TB, D), (1, D, HID), (1, D, HID), (1, HID, D)]
     outs = pl.pallas_call(
         kernel,
-        out_shape=[
-            jax.ShapeDtypeStruct((1, TB, D), BF16),
-            jax.ShapeDtypeStruct((1, TB, D), BF16),
-            jax.ShapeDtypeStruct((D, HID), BF16),
-            jax.ShapeDtypeStruct((D, HID), BF16),
-            jax.ShapeDtypeStruct((HID, D), BF16),
-        ],
+        out_shape=[pltpu.VMEM(shape, BF16) for shape in shapes],
         in_specs=[vmem_spec, vmem_spec, any_spec, any_spec, any_spec],
-        out_specs=[vmem_spec, vmem_spec, any_spec, any_spec, any_spec],
+        out_specs=[vmem_spec] * 5,
         scratch_shapes=[pltpu.VMEM(shape, dtype) for shape, dtype in BUFFERS.values()]
         + [
             pltpu.SemaphoreType.DMA((n,)),
             pltpu.SemaphoreType.DMA((n,)),
             pltpu.SemaphoreType.DMA((3,)),
-            pltpu.SemaphoreType.DMA((3,)),
         ],
         compiler_params=pltpu.CompilerParams(
-            collective_id=0, has_side_effects=True, vmem_limit_bytes=60 << 20
+            collective_id=0, has_side_effects=True, vmem_limit_bytes=46 << 20
         ),
         name="sections",
-    )(inputs, cotangent, gate_weight[0], up_weight[0], down_weight[0])
-    return (outs[0], outs[1], outs[2][None], outs[3][None], outs[4][None])
+    )(inputs, cotangent, gate_weight, up_weight, down_weight)
+    return pl.pallas_call(
+        write_out,
+        out_shape=[jax.ShapeDtypeStruct(shape, BF16) for shape in shapes],
+        in_specs=[vmem_spec] * 5,
+        out_specs=[any_spec] * 5,
+        scratch_shapes=[pltpu.SemaphoreType.DMA((5,))],
+        compiler_params=pltpu.CompilerParams(vmem_limit_bytes=2 << 20),
+        name="write_out",
+    )(*outs)
 
 
 def solution(mesh):

time: 177 us -> 169 us (0.955)
  local copies, waits for them, and re-layouts: 12.5 us -> 0 us
  Pallas kernels: 164 us -> 168 us
    unnamed x9 -> x0, local copies, waits for them, and re-layouts: 12.5 us -> none
    pallas_call x1 -> x2, Pallas kernels: 164 us -> 168 us  [the longest x1 164 us: per_device(): pl.pallas_call(kernel, out_shape=[pltpu.VMEM(shape, BF16) for shape in sh...]
where the time goes in v2:
time: 169 us
  Pallas kernels  168 us (99%)
    pallas_call x1, Pallas kernels, per_device(): pl.pallas_call(kernel, out_shape=[pltpu.VMEM(shape, BF16) for shape in sh...  164 us
    pallas_call x1, Pallas kernels, per_device(): pl.pallas_call(write_out, out_shape=[jax.ShapeDtypeStruct(shape, BF16) fo...  4.36 us

profile of v2, /device:TPU:1, one launch (start us, length us, event | category | flops | bytes accessed | tf_op | source)
XLA Modules:
  0.0 168.8 jit_solution(7594892827752734365)
XLA Ops:
  0.6 163.6 %sections.1 = (bf16[1,48,1024]{2,1,0:T(8,128)(2,1)S(1)}, bf16[1,48,1024]{2,1,0:T(8,128)(2,1)S(1)}, bf16[1,1024,1792]{2,1,0:T(8,128)(2,1)S(1)}, bf16[1,1024,1792]...) custom-call(bf16[48,1024]{1,0:T(8,128)(2,1)} %in_ref.1, bf16[48,1024]{1,0:T(8,128)(2,1)} %ct_ref.1, ...), custom_call_target="tpu_custom_call" | custom-call | tf_op jit(solution)/shard_map/sections/pallas_call | solution.py:439
  164.2 4.4 %write_out.1 = (bf16[1,48,1024]{2,1,0:T(8,128)(2,1)}, bf16[1,48,1024]{2,1,0:T(8,128)(2,1)}, bf16[1,1024,1792]{2,1,0:T(8,128)(2,1)}, bf16[1,1024,1792]{2,1,0:T(8,128)(2,1)}, bf16[1,1792,1024]{2,1,0:T(8,128)(2,1)}) custom-call(bf16[1,48,1024]{2,1,0:T(8,128)(2,1)S(1)} %get-tuple-element.10.refs_0_, bf16[1,48,1024]{2,1,0:T(8,128)(2,1)S(1)} %get-tuple-element.11.refs_1_, ...), custom_call_target="tpu_custom_call" | custom-call | tf_op jit(solution)/shard_map/write_out/pallas_call | solution.py:455
